TPU v7x, 512 devices: a whole 4x4x16 slice. The times are simulated.
512 devices in a mesh: rep: 32 (over z_lo, x), fsdp: 16 (over y, z_hi, core).
Axes of the slice: x: 4, y: 4, z: 16 (z_hi: 2, z_lo: 8; z = z_hi * 8 + z_lo), core: 2. Of those that a mesh axis runs over, the one named last changes fastest.
Arguments:
- hidden_in: bfloat16 [32, 4096, 4096], P('rep', 'fsdp'), may hold values from -6 to 6
- norm_gain: float32 [32, 4096], P('rep'), may hold values from 0.1 to 1.9
- w_value: bfloat16 [32, 4096, 512], P('rep', 'fsdp'), may hold values from -0.09375 to 0.09375
- d_values: bfloat16 [32, 4096, 512], P('rep', 'fsdp'), may hold values from -0.099609375 to 0.099609375
- momentum: float32 [32, 4096, 512], P('rep', 'fsdp'), may hold values from -6 to 6
- step: int32 [], replicated, may hold values from 0 to 63
Outputs:
- values: bfloat16 [32, 4096, 512], P('rep', 'fsdp')
- averaged: float32 [32, 4096, 512], P('rep', 'fsdp')
All inputs are finite; a program needn't handle non-finite values.
Results may differ from a plain program's by a relative error of at most 0.0049.
Values may be sent and summed in bfloat16 or wider, within the bound.
A program may use at most 64 MiB of HBM per device.

v0:
```python
from functools import partial

import jax
import jax.numpy as jnp
from jax import lax
from jax.sharding import PartitionSpec as P


def for_sending(x):

    def short(part):
        return part.astype(jnp.bfloat16) if part.dtype == jnp.float32 else part

    return jax.tree.map(short, x)


def swapped(block, axis, stride):
    count = lax.axis_size(axis)
    route = []
    for low in range(count):
        high = low | 1 << stride
        if high != low and high < count:
            route += [(low, high), (high, low)]
    return lax.ppermute(block, axis, route)


def swap_level(level, state):
    return jax.tree.map(
        lambda part, own: part.astype(own.dtype), swapped(for_sending(state), "rep", level), state
    )


def local(hidden_in, norm_gain, w_value, d_values, momentum, step):
    rows = hidden_in[0].astype(jnp.float32)
    scale = lax.rsqrt(jnp.mean(rows * rows, axis=1, keepdims=True) + 1e-05)
    normed = (rows * scale * norm_gain[0][None, :]).astype(jnp.bfloat16)
    weight = w_value[0]
    cotangent = d_values[0]
    columns_all = lax.all_to_all(normed, "fsdp", split_axis=1, concat_axis=0, tiled=True)
    projected = jnp.dot(
        normed,
        lax.all_gather(weight, "fsdp", axis=0, tiled=True),
        preferred_element_type=jnp.float32,
    )
    grad = lax.dot_general(
        columns_all,
        lax.all_gather(cotangent, "fsdp", axis=0, tiled=True),
        (((0,), (0,)), ((), ())),
        preferred_element_type=jnp.float32,
    )
    updated = 0.9 * momentum[0] + grad
    levels = lax.axis_size("rep").bit_length() - 1
    branches = [partial(swap_level, level) for level in range(levels)]
    partner = lax.switch(step % levels, branches, updated)
    averaged = 0.5 * (updated + partner)
    return (projected.astype(jnp.bfloat16)[None], averaged[None])


def solution(mesh):
    placed = (
        P("rep", "fsdp", None),
        P("rep", None),
        P("rep", "fsdp", None),
        P("rep", "fsdp", None),
        P("rep", "fsdp", None),
        P(),
    )
    return jax.shard_map(
        local,
        mesh=mesh,
        in_specs=placed,
        out_specs=(P("rep", "fsdp", None), P("rep", "fsdp", None)),
        check_vma=False,
    )
```

profile of v0, /device:TPU:1, one launch (start us, length us, event | category | flops | bytes accessed | tf_op | source)
XLA Modules:
  0.0 331.8 jit_solution(17564587072228424425)
XLA Ops:
  7.2 0.0 copy-start
  7.2 0.0 all-gather.7.cloned.1.call-start
  7.2 0.7 all-gather.7.cloned.1.call-update
  7.9 3.3 copy.8
  11.2 0.5 broadcast.22
  11.7 0.0 copy-done
  11.7 0.7 reduce.3
  12.4 0.6 fusion.4
  13.0 1.7 multiply_convert_fusion
  14.7 0.0 copy-start.1
  14.7 19.4 %all-to-all-start = ((bf16[256,16,256]{0,2,1:T(8,128)(2,1)}), bf16[256,16,256]{0,2,1:T(8,128)(2,1)}, u32[]{:S(2)}, u32[]{:S(2)}) async-start(bf16[256,16,256]{0,2,1:T(8,128)(2,1)} %multiply_convert_fusion), calls=%async_computation | async-start | bytes 4194304 | tf_op jit(solution)/shard_map/all_to_all | solution.py:39
  34.1 0.0 all-gather.5.cloned.1.call-start
  34.1 0.7 all-gather.5.cloned.1.call-update
  35.5 67.8 %all-to-all-done = bf16[256,16,256]{0,2,1:T(8,128)(2,1)} async-done(((bf16[256,16,256]{0,2,1:T(8,128)(2,1)}), bf16[256,16,256]{0,2,1:T(8,128)(2,1)}, u32[]{:S(2)}, u32[]{:S(2)}) %all-to-all-start) | async-done | bytes 2097184 | tf_op jit(solution)/shard_map/all_to_all | solution.py:39
  103.3 3.9 %copy.9 = bf16[16,256,256]{2,1,0:T(8,128)(2,1)} copy(bf16[16,256,256]{1,2,0:T(8,128)(2,1)} %bitcast.6) | data formatting | bytes 4194304 | tf_op jit(solution)/shard_map/all_to_all | solution.py:39
  107.2 91.4 %all-gather.7.cloned.1.call-done = bf16[1,4096,512]{2,1,0:T(8,128)(2,1)} async-done(((bf16[1,256,512]{2,1,0:T(8,128)(2,1)}), bf16[1,4096,512]{2,1,0:T(8,128)(2,1)}) %all-gather.7.cloned.1.call-update) | async-done | bytes 4194320 | tf_op jit(solution)/shard_map/all_gather | solution.py:47
  198.6 0.0 copy-done.1
  198.6 4.1 %fusion.11 = f32[256,512]{1,0:T(8,128)S(1)} fusion(bf16[4096,256]{1,0:T(8,128)(2,1)} %bitcast.39, bf16[1,4096,512]{2,1,0:T(8,128)(2,1)} %all-gather.7.cloned.1.call-done, f32[1,256,512]{2,1,0:T(8,128)S(1)} %copy-done.1), kind=kOutput, calls=%fused_computation.13 | convolution fusion | flops 1074003968 | bytes 7340032 | tf_op jit(solution)/shard_map/dot_general | solution.py:45
  202.7 10.6 %conditional.4 = (f32[256,512]{1,0:T(8,128)S(1)}) conditional(s32[]{:T(128)} %clamp.3, f32[256,512]{1,0:T(8,128)S(1)} %fusion.11, f32[256,512]{1,0:T(8,128)S(1)} %fusion.11, f32[256,512]{1,0:T(8,128)S(1)} %fusion.11, f32[256,512]{1,0:T(8,128)S(1)} %fusion.11, f32[256,512]{1,0:T(8,128)S(1)} %fusion.11), branch_computations={%region_1.2_spmd, %region_2.3_spmd, %region_3.4_spmd, %region_4.5_... | conditional | flops 262144 | bytes 2621488
  202.8 3.3 collective-permute-start.3
  206.1 7.2 %collective-permute-done.3 = bf16[256,512]{1,0:T(8,128)(2,1)S(1)} collective-permute-done((bf16[256,512]{1,0:T(8,128)(2,1)S(1)}, bf16[256,512]{1,0:T(8,128)(2,1)S(1)}, u32[]{:S(2)}, u32[]{:S(2)}) %collective-permute-start.3) | collective-permute-done | bytes 262176 | tf_op jit(solution)/shard_map/cond/branch_3_fun/ppermute | solution.py:24
  213.3 0.9 multiply_bitcast_fusion
  214.2 105.4 %all-gather.5.cloned.1.call-done = bf16[1,4096,512]{2,1,0:T(8,128)(2,1)} async-done(((bf16[1,256,512]{2,1,0:T(8,128)(2,1)}), bf16[1,4096,512]{2,1,0:T(8,128)(2,1)}) %all-gather.5.cloned.1.call-update) | async-done | bytes 4194320 | tf_op jit(solution)/shard_map/all_gather | solution.py:42
  319.6 5.4 %fusion.19 = bf16[1,256,512]{2,1,0:T(8,128)(2,1)} fusion(bf16[1,4096,512]{2,1,0:T(8,128)(2,1)} %all-gather.5.cloned.1.call-done, bf16[1,256,4096]{1,2,0:T(8,128)(2,1)S(1)} %copy.8, f32[4096]{0:T(1024)S(1)} %bitcast.40, f32[256]{0:T(256)S(1)} %add_rsqrt_fusion), kind=kOutput, calls=%fused_computation.15 | convolution fusion | flops 1078067200 | bytes 6571008 | tf_op jit(solution)/shard_map/dot_general | solution.py:40
  (4 shorter events, 0.1 us)
Async XLA Ops:
  7.2 4.5 %copy-start = (f32[1,4096]{1,0:T(1,128)S(1)}, f32[1,4096]{1,0:T(1,128)}, u32[]{:S(2)}) copy-start(f32[1,4096]{1,0:T(1,128)} %param.12) | copy-start | bytes 49156
  7.2 191.4 %all-gather.7.cloned.1.call-start = ((), (), s32[]{:S(2)}) async-start(), calls=%async_computation.2 | async-start | bytes 4456448 | tf_op jit(solution)/shard_map/all_gather | solution.py:47
  14.7 183.9 %copy-start.1 = (f32[1,256,512]{2,1,0:T(8,128)S(1)}, f32[1,256,512]{2,1,0:T(8,128)}, u32[]{:S(2)}) copy-start(f32[1,256,512]{2,1,0:T(8,128)} %param.15) | copy-start | bytes 1572868
  14.7 88.6 %all-to-all-start = ((bf16[256,16,256]{0,2,1:T(8,128)(2,1)}), bf16[256,16,256]{0,2,1:T(8,128)(2,1)}, u32[]{:S(2)}, u32[]{:S(2)}) async-start(bf16[256,16,256]{0,2,1:T(8,128)(2,1)} %multiply_convert_fusion), calls=%async_computation | async-start | bytes 4194304 | tf_op jit(solution)/shard_map/all_to_all | solution.py:39
  34.1 285.5 %all-gather.5.cloned.1.call-start = ((), (), s32[]{:S(2)}) async-start(), calls=%async_computation.1 | async-start | bytes 4456448 | tf_op jit(solution)/shard_map/all_gather | solution.py:42
  202.8 10.4 %collective-permute-start.3 = (bf16[256,512]{1,0:T(8,128)(2,1)S(1)}, bf16[256,512]{1,0:T(8,128)(2,1)S(1)}, u32[]{:S(2)}, u32[]{:S(2)}) collective-permute-start(bf16[256,512]{1,0:T(8,128)(2,1)S(1)} %convert_element_type.52), channel_id=1, source_target_pairs={{0,128},{128,0},{16,144},{144,16},{32,160},{160,32},{48,176},{176,... | collective-permute-start | bytes 786440 | tf_op jit(solution)/shard_map/cond/branch_3_fun/ppermute | solution.py:24
Sparse Core Ops, SparseCore 0:
  11.3 187.2 all-gather.6
  201.9 117.6 all-gather.4
where the time goes:
time: 332 us
  waiting for transfers between devices  273 us (82%)
  starting transfers between devices  22.7 us (7%)
  between operations  14.8 us (4%)
  matrix products  9.47 us (3%)
  local copies, waits for them, and re-layouts  7.73 us (2%)
  other arithmetic  3.94 us (1%)
    all_gather x1, waiting for transfers between devices, local(): lax.all_gather(weight, 'fsdp', axis=0, tiled=True)  105 us
    all_gather x1, waiting for transfers between devices, local(): lax.all_gather(cotangent, 'fsdp', axis=0, tiled=True)  91.4 us
    all_to_all x1, waiting for transfers between devices, local(): lax.all_to_all(normed, 'fsdp', split_axis=1, concat_axis=0, tiled=True)  67.8 us
    all_to_all x1, starting transfers between devices, local(): lax.all_to_all(normed, 'fsdp', split_axis=1, concat_axis=0, tiled=True)  19.4 us
    ppermute x1, waiting for transfers between devices, swapped(): return lax.ppermute(block, axis, route)  7.18 us
  transfers between devices with their start and end apart: 4, of which 4 were waited for; matrix products, arithmetic and copies ran while one was open for 5% of the time, Pallas kernels for 0%

commit v1 on v0

v1 whole, which is shorter than its diff:
```python
from functools import partial

import jax
import jax.numpy as jnp
from jax import lax
from jax.experimental import pallas as pl
from jax.experimental.pallas import tpu as pltpu
from jax.sharding import PartitionSpec as P

MESH = pl.DeviceIdType.MESH
F32 = jnp.float32
BF16 = jnp.bfloat16
N_Y = 4
W_CHUNKS = 4


def kernel(
    level, hid_ref, gain_ref, w_ref, d_ref, mom_ref, values_ref, averaged_ref,
    hid, d_own, mom, normed, to_core, dt, wts, part, vals_in, vals_out,
    g_out, g_in, g_sum, z_out, z_in, x_out, x_in, avg,
    local_sem, send_sem, recv_sem,
):
    rows, feats = hid.shape
    kv = d_own.shape[1]
    blk = w_ref.shape[0]
    rep, shard = lax.axis_index("rep"), lax.axis_index("fsdp")
    core = shard % 2
    half = (shard // 2) % 2
    y = shard // 4

    def at(r, yy, hh, cc):
        return (r, (yy * 2 + hh) * 2 + cc)

    bit = (rep // 2**level) % 2
    pair_rep = rep + (1 - 2 * bit) * 2**level
    y_dev = [None] + [at(rep, (y + k) % N_Y, half, core) for k in range(1, N_Y)]
    z_dev = at(rep, y, 1 - half, core)
    core_dev = at(rep, y, half, 1 - core)
    pair_dev = at(pair_rep, y, half, core)
    cross_dev = z_dev if level < 2 else at(pair_rep, y, 1 - half, core)
    friends = y_dev[1:] + [z_dev, core_dev, pair_dev]
    if level >= 2:
        friends = friends + [cross_dev]

    barrier = pltpu.get_barrier_semaphore()
    for device in friends:
        pl.semaphore_signal(barrier, 1, device_id=device, device_id_type=MESH)

    def fetch(src, dst, i):
        copy = pltpu.make_async_copy(src, dst, local_sem.at[i])
        copy.start()
        return copy

    load_hid = fetch(hid_ref, hid, 0)
    load_d = fetch(d_ref, d_own, 1)
    load_w = fetch(w_ref, wts.at[0], 2)
    load_mom = fetch(mom_ref, mom, 3)

    counter = [0]

    def send(src, dst, device):
        i = counter[0]
        counter[0] += 1
        copy = pltpu.make_async_remote_copy(
            src, dst, send_sem.at[i], recv_sem.at[i], device_id=device, device_id_type=MESH
        )
        copy.start()
        return copy

    load_d.wait()
    dt[0] = d_own[...].astype(F32).T.astype(BF16)
    load_hid.wait()
    step = 32

    def norm_rows(i, carry):
        here = pl.ds(pl.multiple_of(i * step, step), step)
        total = jnp.zeros((step, blk), F32)
        for j in range(feats // blk):
            x = hid[here, j * blk : (j + 1) * blk].astype(F32)
            total = total + x * x
        scale = lax.rsqrt(jnp.sum(total, axis=1, keepdims=True) * (1.0 / feats) + 1e-05)
        for j in range(feats // (2 * blk)):
            for mine in range(2):
                which = core if mine else 1 - core
                cols = pl.ds(pl.multiple_of((2 * j + which) * blk, blk), blk)
                out = (hid[here, cols].astype(F32) * scale * gain_ref[:, cols]).astype(BF16)
                if mine:
                    normed[0, here, j * blk : (j + 1) * blk] = out
                else:
                    to_core[here, j * blk : (j + 1) * blk] = out
        return carry

    lax.fori_loop(0, rows // step, norm_rows, 0)

    pl.semaphore_wait(barrier, len(friends))

    piece = blk // W_CHUNKS
    w_cross = []
    for q in range(W_CHUNKS):
        span = pl.ds(q * piece, piece)
        w_cross.append(send(w_ref.at[span], wts.at[4, span], z_dev))
    core_d = send(dt.at[0], dt.at[1], core_dev)
    core_n = send(to_core, normed.at[1], core_dev)
    w_y = [None] + [send(w_ref, wts.at[N_Y - k], y_dev[k]) for k in range(1, N_Y)]

    def block(k, far):
        hh = 1 - half if far else half
        return pl.multiple_of((((y + k) % N_Y) * 2 + hh) * blk, blk)

    def grad_block(k, far):
        cols = pl.ds(block(k, far), blk)
        return jnp.dot(dt[0], normed[0, :, cols], preferred_element_type=F32) + jnp.dot(
            dt[1], normed[1, :, cols], preferred_element_type=F32
        )

    core_d.wait_recv()
    core_n.wait_recv()
    g_sent = {}
    for far in (1, 0):
        for k in (2, 1, 3):
            slot = far * 3 + k - 1
            g_out[slot] = grad_block(k, far).astype(BF16)
            g_sent[far, k] = send(g_out.at[slot], g_in.at[slot], y_dev[k])
        g_sum[far] = grad_block(0, far)

    def project(k, far, first=False):
        cols = pl.ds(block(k, far), blk)
        for t in range(2):
            new = jnp.dot(normed[t, :, cols], wts[4 * far + k], preferred_element_type=F32)
            part[t] = new if first else part[t] + new

    load_w.wait()
    project(0, 0, True)
    for k in range(1, N_Y):
        w_y[k].wait_recv()
        project(N_Y - k, 0)

    for k in range(1, N_Y):
        g_sent[1, k].wait_recv()
    z_out[...] = (
        g_sum[1] + g_in[3].astype(F32) + g_in[4].astype(F32) + g_in[5].astype(F32)
    ).astype(BF16)
    g_cross = send(z_out, z_in, cross_dev)

    forwards = []
    for q in range(W_CHUNKS):
        span = pl.ds(q * piece, piece)
        w_cross[q].wait_recv()
        for k in range(1, N_Y):
            forwards.append((k, send(wts.at[4, span], wts.at[4 + N_Y - k, span], y_dev[k])))
    project(0, 1)

    for k in range(1, N_Y):
        g_sent[0, k].wait_recv()
    load_mom.wait()
    g_sum[0] = g_sum[0] + g_in[0].astype(F32) + g_in[1].astype(F32) + g_in[2].astype(F32)

    for k in range(1, N_Y):
        for kk, copy in forwards:
            if kk == k:
                copy.wait_recv()
        project(N_Y - k, 1)
    vals_send = send(part.at[1], vals_in, core_dev)
    vals_send.wait_recv()
    vals_out[...] = (part[0] + vals_in[...]).astype(BF16)
    store_vals = fetch(vals_out, values_ref, 4)

    g_cross.wait_recv()
    updated = 0.9 * mom[...] + (g_sum[0] + z_in[...].astype(F32)).T
    avg[...] = updated
    x_out[...] = updated.astype(BF16)
    x_send = send(x_out, x_in, pair_dev)
    x_send.wait_recv()
    avg[...] = 0.5 * (avg[...] + x_in[...].astype(F32))
    store_avg = fetch(avg, averaged_ref, 5)

    for copy in w_cross + w_y[1:] + [core_d, core_n, g_cross, vals_send, x_send]:
        copy.wait_send()
    for copy in g_sent.values():
        copy.wait_send()
    for _, copy in forwards:
        copy.wait_send()
    store_vals.wait()
    store_avg.wait()


def fused(level, hidden, gain, weight, cotangent, momentum):
    rows, feats = hidden.shape
    blk, kv = weight.shape
    copies = W_CHUNKS * N_Y + 2 + 3 + 6 + 1 + 1 + 1
    anywhere = pl.BlockSpec(memory_space=pl.ANY)
    return pl.pallas_call(
        partial(kernel, level),
        name=f"layer_level_{level}",
        out_shape=(
            jax.ShapeDtypeStruct((rows, kv), BF16),
            jax.ShapeDtypeStruct((blk, kv), F32),
        ),
        in_specs=[
            anywhere,
            pl.BlockSpec(memory_space=pltpu.VMEM),
            anywhere,
            anywhere,
            anywhere,
        ],
        out_specs=(anywhere, anywhere),
        scratch_shapes=[
            pltpu.VMEM((rows, feats), BF16),
            pltpu.VMEM((rows, kv), BF16),
            pltpu.VMEM((blk, kv), F32),
            pltpu.VMEM((2, rows, feats // 2), BF16),
            pltpu.VMEM((rows, feats // 2), BF16),
            pltpu.VMEM((2, kv, rows), BF16),
            pltpu.VMEM((8, blk, kv), BF16),
            pltpu.VMEM((2, rows, kv), F32),
            pltpu.VMEM((rows, kv), F32),
            pltpu.VMEM((rows, kv), BF16),
            pltpu.VMEM((6, kv, blk), BF16),
            pltpu.VMEM((6, kv, blk), BF16),
            pltpu.VMEM((2, kv, blk), F32),
            pltpu.VMEM((kv, blk), BF16),
            pltpu.VMEM((kv, blk), BF16),
            pltpu.VMEM((blk, kv), BF16),
            pltpu.VMEM((blk, kv), BF16),
            pltpu.VMEM((blk, kv), F32),
            pltpu.SemaphoreType.DMA((6,)),
            pltpu.SemaphoreType.DMA((copies,)),
            pltpu.SemaphoreType.DMA((copies,)),
        ],
        compiler_params=pltpu.CompilerParams(
            collective_id=level, has_side_effects=True, vmem_limit_bytes=40 << 20
        ),
    )(hidden, gain, weight, cotangent, momentum)


def local(hidden_in, norm_gain, w_value, d_values, momentum, step):
    levels = lax.axis_size("rep").bit_length() - 1
    branches = [partial(fused, level) for level in range(levels)]
    values, averaged = lax.switch(
        step % levels, branches, hidden_in[0], norm_gain, w_value[0], d_values[0], momentum[0]
    )
    return (values[None], averaged[None])


def solution(mesh):
    placed = (
        P("rep", "fsdp", None),
        P("rep", None),
        P("rep", "fsdp", None),
        P("rep", "fsdp", None),
        P("rep", "fsdp", None),
        P(),
    )
    return jax.shard_map(
        local,
        mesh=mesh,
        in_specs=placed,
        out_specs=(P("rep", "fsdp", None), P("rep", "fsdp", None)),
        check_vma=False,
    )
```

time: 332 us -> 78.2 us (0.24)
  waiting for transfers between devices: 273 us -> 0 us
  Pallas kernels: 0 us -> 75 us
  starting transfers between devices: 22.7 us -> 0 us
  between operations: 14.8 us -> 1.3 us
  matrix products: 9.47 us -> 0 us
  local copies, waits for them, and re-layouts: 7.73 us -> 1.5 us
  other arithmetic: 3.94 us -> 0 us
    all_gather x2 -> x0, waiting for transfers between devices: 197 us -> none  [the longest x1 105 us: local(): lax.all_gather(weight, 'fsdp', axis=0, tiled=True)]
    pallas_call x0 -> x1, Pallas kernels: none -> 75 us  [fused(): pl.pallas_call(partial(kernel, level), name=f'layer_level_{level}', out_s...]
    all_to_all x1 -> x0, waiting for transfers between devices: 67.8 us -> none  [local(): lax.all_to_all(normed, 'fsdp', split_axis=1, concat_axis=0, tiled=True)]
    all_to_all x1 -> x0, starting transfers between devices: 19.4 us -> none  [local(): lax.all_to_all(normed, 'fsdp', split_axis=1, concat_axis=0, tiled=True)]
    dot_general x2 -> x0, matrix products: 9.47 us -> none  [the longest x1 5.39 us: local(): jnp.dot(normed, lax.all_gather(weight, 'fsdp', axis=0, tiled=True), prefe...]
    ppermute x1 -> x0, waiting for transfers between devices: 7.18 us -> none  [swapped(): return lax.ppermute(block, axis, route)]
    all_to_all x1 -> x0, local copies, waits for them, and re-layouts: 3.92 us -> none  [local(): lax.all_to_all(normed, 'fsdp', split_axis=1, concat_axis=0, tiled=True)]
  transfers between devices with their start and end apart: 4 -> 0, of which waited for: 4 -> 0; matrix products, arithmetic and copies ran while one was open for 5% -> 0% of each run, Pallas kernels for 0% -> 0%
where the time goes in v1:
time: 78.2 us; the launch traced here: 78 us
  Pallas kernels  75 us (96%)
  local copies, waits for them, and re-layouts  1.5 us (2%)
  between operations  1.3 us (2%)
    pallas_call x1, Pallas kernels, fused(): pl.pallas_call(partial(kernel, level), name=f'layer_level_{level}', out_s...  75 us

profile of v1, /device:TPU:1, one launch (start us, length us, event | category | flops | bytes accessed | tf_op | source)
XLA Modules:
  0.0 78.0 jit_solution(14181440158951102876)
XLA Ops:
  1.3 75.2 %conditional.1 = ((bf16[256,512]{1,0:T(8,128)(2,1)S(1)}, f32[256,512]{1,0:T(8,128)S(1)})) conditional(s32[]{:T(128)} %clamp.3, (bf16[256,4096]{1,0:T(8,128)(2,1)}, f32[1,4096]{1,0:T(1,128)}, bf16[256,512]{1,0:T(8,128)(2,1)}, bf16[256,512]{1,0:T(8,128)(2,1)}, f32[256,512]{1,0:T(8,128)}) %tuple.71, ...), branch_computations={%region_0.1_spmd, %region_1.2_spmd, %region_2.3_spmd, %region_3.4_... | conditional | bytes 8 | solution.py:239
  1.3 75.0 %layer_level_2.1 = (bf16[256,512]{1,0:T(8,128)(2,1)S(1)}, f32[256,512]{1,0:T(8,128)S(1)}) custom-call(bf16[256,4096]{1,0:T(8,128)(2,1)} %get-tuple-element.76.hid_ref, f32[1,4096]{1,0:T(1,128)} %get-tuple-element.77.gain_ref, bf16[256,512]{1,0:T(8,128)(2,1)} %get-tuple-element.78.w_ref, bf16[256,512]{1,0:T(8,128)(2,1)} %get-tuple-element.79.d_ref, ...), custom_call_target="tpu_custom_call" | custom-call | tf_op jit(solution)/shard_map/cond/branch_2_fun/layer_level_2/pallas_call | solution.py:192
  76.5 0.7 copy.21
  77.2 0.8 %copy.22 = f32[1,256,512]{2,1,0:T(8,128)} copy(f32[1,256,512]{2,1,0:T(8,128)S(1)} %bitcast.26) | data formatting | bytes 1048576

commit v2 on v0

v2 whole, which is shorter than its diff:
```python
from functools import partial

import jax
import jax.numpy as jnp
from jax import lax
from jax.experimental import pallas as pl
from jax.experimental.pallas import tpu as pltpu
from jax.sharding import PartitionSpec as P

MESH = pl.DeviceIdType.MESH
F32 = jnp.float32
BF16 = jnp.bfloat16
N_X = 4
N_Y = 4
X_LEVELS = 2
W_CHUNKS = 4
BACK = 2


def copies_of(level):
    common = W_CHUNKS + 4 + 6 + 3 * W_CHUNKS + BACK
    return common + (22 + BACK if level < X_LEVELS else 12 + 3 * BACK)


def kernel(
    level, hid_ref, gain_ref, w_ref, d_ref, mom_ref, values_ref, averaged_ref,
    hid, mom, normed, to_core, d, wts, part, vals_in,
    keep, keep_side, first_out, first_in, side_out, side_in, own_out, own_in,
    z_out, z_in, back_out, back_in,
    local_sem, send_sem, recv_sem,
):
    along_x = level < X_LEVELS
    rows, feats = hid.shape
    blk, kv = w_ref.shape
    mid, cols = blk // 2, kv // 2
    rep, shard = lax.axis_index("rep"), lax.axis_index("fsdp")
    y, half, core = shard // 4, (shard // 2) % 2, shard % 2

    def at(r, yy, hh, cc):
        return (r, (((yy + N_Y) % N_Y) * 2 + hh) * 2 + cc)

    bit = (rep // 2**level) % 2
    pair_rep = rep + (1 - 2 * bit) * 2**level
    up, down = at(rep, y + 1, half, core), at(rep, y - 1, half, core)
    across = at(rep, y, 1 - half, core)
    other = at(rep, y, half, 1 - core)
    pair = at(pair_rep, y, half, core)
    friends = [up, down, across, other, pair]
    if along_x:
        pair_up, pair_down = at(pair_rep, y + 1, half, core), at(pair_rep, y - 1, half, core)
        friends = friends + [pair_up, pair_down]
    else:
        pair_across = at(pair_rep, y, 1 - half, core)
        friends = friends + [pair_across]

    barrier = pltpu.get_barrier_semaphore()
    for device in friends:
        pl.semaphore_signal(barrier, 1, device_id=device, device_id_type=MESH)

    def fetch(src, dst, i):
        copy = pltpu.make_async_copy(src, dst, local_sem.at[i])
        copy.start()
        return copy

    load_hid = fetch(hid_ref, hid, 0)
    load_d = fetch(d_ref, d.at[0], 1)

    sent = []

    def send(src, dst, device):
        i = len(sent)
        copy = pltpu.make_async_remote_copy(
            src, dst, send_sem.at[i], recv_sem.at[i], device_id=device, device_id_type=MESH
        )
        copy.start()
        sent.append(copy)
        return copy

    pl.semaphore_wait(barrier, len(friends))

    def piece(q):
        n = blk // W_CHUNKS
        return pl.ds(q * n, n)

    w_cross = [send(w_ref.at[piece(q)], wts.at[4, piece(q)], across) for q in range(W_CHUNKS)]
    load_w = fetch(w_ref, wts.at[0], 2)
    load_mom = fetch(mom_ref, mom, 3)
    load_d.wait()
    core_d = send(d.at[0], d.at[1], other)

    step = 32

    def norm_rows(i, carry):
        here = pl.ds(pl.multiple_of(i * step, step), step)
        total = jnp.zeros((step, blk), F32)
        for j in range(feats // blk):
            v = hid[here, j * blk : (j + 1) * blk].astype(F32)
            total = total + v * v
        scale = lax.rsqrt(jnp.sum(total, axis=1, keepdims=True) * (1.0 / feats) + 1e-05)
        for j in range(2 * N_Y):
            for mine in range(2):
                which = core if mine else 1 - core
                span = pl.ds(pl.multiple_of((2 * j + which) * blk, blk), blk)
                out = (hid[here, span].astype(F32) * scale * gain_ref[:, span]).astype(BF16)
                if mine:
                    normed[0, j % 2, j // 2, here] = out
                else:
                    to_core[j % 2, j // 2, here] = out
        return carry

    load_hid.wait()
    lax.fori_loop(0, rows // step, norm_rows, 0)
    core_n = {
        1: send(to_core.at[1 - half], normed.at[1, 1 - half], other),
        0: send(to_core.at[half], normed.at[1, half], other),
    }

    def tokens_of(t, k, far):
        return normed[t, 1 - half if far else half, (y + k) % N_Y]

    def grad_block(k, far):
        return sum(
            lax.dot_general(
                tokens_of(t, k, far), d[t], (((0,), (0,)), ((), ())), preferred_element_type=F32
            )
            for t in range(2)
        )

    mine = pl.ds(pl.multiple_of(bit * mid, mid), mid)
    theirs = pl.ds(pl.multiple_of((1 - bit) * mid, mid), mid)
    first, side, own = {}, {0: [], 1: []}, {}

    def send_side(far, way, part_of):
        src = side_out.at[far, way, part_of]
        if along_x:
            ends = ((up, down)[way], (pair_up, pair_down)[way])
            for i, span in enumerate((mine, theirs)):
                side[far].append(
                    send(src.at[span], side_in.at[far, way, part_of, pl.ds(i * mid, mid)], ends[i])
                )
        else:
            side[far].append(send(src, side_in.at[far, way, part_of], (up, down)[way]))

    def reduce_first(far):
        block = grad_block(2, far).astype(BF16)
        first_out[far, 0] = block[:, :cols]
        first_out[far, 1] = block[:, cols:]
        first[far] = [
            send(first_out.at[far, 0], first_in.at[far, 0], up),
            send(first_out.at[far, 1], first_in.at[far, 1], down),
        ]
        for way, k in ((0, 1), (1, 3)):
            block = grad_block(k, far)
            parts = (block[:, :cols], block[:, cols:])
            side_out[far, way, 1 - way] = parts[1 - way].astype(BF16)
            send_side(far, way, 1 - way)
            keep_side[far, way] = parts[way]
        block = grad_block(0, far)
        if not far:
            block = block + 0.9 * mom[...]
        keep[far] = block
        if along_x:
            own_out[far] = keep[far, theirs].astype(BF16)
            own[far] = send(own_out.at[far], own_in.at[far], pair)

    def reduce_second(far):
        for way in range(2):
            first[far][way].wait_recv()
            side_out[far, way, way] = (
                keep_side[far, way] + first_in[far, way].astype(F32)
            ).astype(BF16)
            send_side(far, way, way)

    def reduced(far, span, copies):
        total = keep[far, span]
        for at_row in copies:
            for way in range(2):
                total = total + jnp.concatenate(
                    [side_in[far, way, c, pl.ds(at_row, mid)] for c in range(2)], axis=1
                ).astype(F32)
        return total

    def wait_reduced(far):
        for copy in side[far]:
            copy.wait_recv()
        if along_x:
            own[far].wait_recv()

    def project(k, far, begin=False, tokens=(0, 1)):
        for t in tokens:
            new = jnp.dot(tokens_of(t, k, far), wts[4 * far + k], preferred_element_type=F32)
            part[t] = new if begin else part[t] + new

    def back_rows(i):
        n = mid // BACK
        return pl.ds(i * n, n)

    core_d.wait_recv()
    core_n[1].wait_recv()
    reduce_first(1)
    core_n[0].wait_recv()
    load_w.wait()
    load_mom.wait()
    project(0, 0, True)
    reduce_second(1)
    reduce_first(0)

    wait_reduced(1)
    crossing = []
    if along_x:
        z_out[0] = (reduced(1, mine, (0, mid)) + own_in[1].astype(F32)).astype(BF16)
        for i in range(BACK):
            crossing.append(send(z_out.at[0, back_rows(i)], z_in.at[0, back_rows(i)], across))
    else:
        for i, span in enumerate((mine, theirs)):
            start = bit * mid if i == 0 else (1 - bit) * mid
            z_out[i] = reduced(1, span, (pl.multiple_of(start, mid),)).astype(BF16)
        for q in range(BACK):
            for i, device in enumerate((across, pair_across)):
                crossing.append(send(z_out.at[i, back_rows(q)], z_in.at[i, back_rows(q)], device))

    far_up, far_down, far_relay = {}, {}, []

    def spread(q):
        w_cross[q].wait_recv()
        s = piece(q)
        for way in (q % 2, 1 - q % 2):
            if way == 0:
                far_up[q] = send(wts.at[4, s], wts.at[7, s], up)
            else:
                far_down[q] = send(wts.at[4, s], wts.at[5, s], down)

    def relay(q):
        s = piece(q)
        if q % 2 == 0:
            far_up[q].wait_recv()
            far_relay.append(send(wts.at[7, s], wts.at[6, s], up))
        else:
            far_down[q].wait_recv()
            far_relay.append(send(wts.at[5, s], wts.at[6, s], down))

    spread(0)
    reduce_second(0)
    lower, upper = pl.ds(0, mid), pl.ds(mid, mid)
    near_up = [send(w_ref.at[s], wts.at[3, s], up) for s in (lower, upper)]
    near_down = [send(w_ref.at[s], wts.at[1, s], down) for s in (upper, lower)]
    spread(1)
    relay(0)
    wait_reduced(0)
    pair_near = []
    if along_x:
        keep[0, mine] = reduced(0, mine, (0, mid)) + own_in[0].astype(F32)
    else:
        z_out[2] = reduced(0, theirs, (pl.multiple_of((1 - bit) * mid, mid),)).astype(BF16)
        for q in range(BACK):
            pair_near.append(send(z_out.at[2, back_rows(q)], z_in.at[2, back_rows(q)], pair))
        keep[0, mine] = reduced(0, mine, (pl.multiple_of(bit * mid, mid),))
    near_up[0].wait_recv()
    near_down[0].wait_recv()
    near_relay = [
        send(wts.at[3, lower], wts.at[2, lower], up),
        send(wts.at[1, upper], wts.at[2, upper], down),
    ]
    spread(2)
    relay(1)
    near_up[1].wait_recv()
    near_down[1].wait_recv()
    project(1, 0)
    project(3, 0)
    spread(3)
    relay(2)
    project(0, 1)
    relay(3)
    for copy in near_relay:
        copy.wait_recv()
    project(2, 0)
    for q in range(W_CHUNKS):
        if q % 2 == 0:
            far_down[q].wait_recv()
        else:
            far_up[q].wait_recv()
    project(1, 1)
    project(3, 1)

    back = []

    def finish(q):
        s = back_rows(q)
        n = mid // BACK
        total = keep[0, pl.ds(pl.multiple_of(bit * mid + q * n, n), n)]
        if along_x:
            crossing[q].wait_recv()
            total = total + z_in[0, s].astype(F32)
        else:
            crossing[2 * q].wait_recv()
            crossing[2 * q + 1].wait_recv()
            pair_near[q].wait_recv()
            total = total + z_in[0, s].astype(F32) + z_in[1, s].astype(F32) + z_in[2, s].astype(F32)
        result = 0.5 * total
        back_out[s] = result.astype(BF16)
        back.append(send(back_out.at[s], back_in.at[s], pair))
        averaged_ref[pl.ds(pl.multiple_of(bit * mid + q * n, n), n)] = result

    for copy in far_relay:
        copy.wait_recv()
    project(2, 1, tokens=(1,))
    vals_send = send(part.at[1], vals_in, other)
    project(2, 1, tokens=(0,))
    for q in range(BACK):
        finish(q)
    vals_send.wait_recv()
    values_ref[...] = (part[0] + vals_in[...]).astype(BF16)
    for copy in back:
        copy.wait_recv()
    averaged_ref[theirs] = back_in[...].astype(F32)

    assert len(sent) == copies_of(level)
    for copy in sent:
        copy.wait_send()


def fused(level, hidden, gain, weight, cotangent, momentum):
    rows, feats = hidden.shape
    blk, kv = weight.shape
    mid, cols = blk // 2, kv // 2
    anywhere = pl.BlockSpec(memory_space=pl.ANY)
    vmem = pl.BlockSpec(memory_space=pltpu.VMEM)
    return pl.pallas_call(
        partial(kernel, level),
        name=f"layer_level_{level}",
        out_shape=(
            jax.ShapeDtypeStruct((rows, kv), BF16),
            jax.ShapeDtypeStruct((blk, kv), F32),
        ),
        in_specs=[anywhere, vmem, anywhere, anywhere, anywhere],
        out_specs=(vmem, vmem),
        scratch_shapes=[
            pltpu.VMEM((rows, feats), BF16),
            pltpu.VMEM((blk, kv), F32),
            pltpu.VMEM((2, 2, N_Y, rows, blk), BF16),
            pltpu.VMEM((2, N_Y, rows, blk), BF16),
            pltpu.VMEM((2, rows, kv), BF16),
            pltpu.VMEM((2 * N_Y, blk, kv), BF16),
            pltpu.VMEM((2, rows, kv), F32),
            pltpu.VMEM((rows, kv), F32),
            pltpu.VMEM((2, blk, kv), F32),
            pltpu.VMEM((2, 2, blk, cols), F32),
            pltpu.VMEM((2, 2, blk, cols), BF16),
            pltpu.VMEM((2, 2, blk, cols), BF16),
            pltpu.VMEM((2, 2, 2, blk, cols), BF16),
            pltpu.VMEM((2, 2, 2, blk, cols), BF16),
            pltpu.VMEM((2, mid, kv), BF16),
            pltpu.VMEM((2, mid, kv), BF16),
            pltpu.VMEM((3, mid, kv), BF16),
            pltpu.VMEM((3, mid, kv), BF16),
            pltpu.VMEM((mid, kv), BF16),
            pltpu.VMEM((mid, kv), BF16),
            pltpu.SemaphoreType.DMA((4,)),
            pltpu.SemaphoreType.DMA((copies_of(level),)),
            pltpu.SemaphoreType.DMA((copies_of(level),)),
        ],
        compiler_params=pltpu.CompilerParams(
            collective_id=level, has_side_effects=True, vmem_limit_bytes=40 << 20
        ),
    )(hidden, gain, weight, cotangent, momentum)


def local(hidden_in, norm_gain, w_value, d_values, momentum, step):
    levels = lax.axis_size("rep").bit_length() - 1
    branches = [partial(fused, level) for level in range(levels)]
    values, averaged = lax.switch(
        step % levels, branches, hidden_in[0], norm_gain, w_value[0], d_values[0], momentum[0]
    )
    return (values[None], averaged[None])


def solution(mesh):
    placed = (
        P("rep", "fsdp", None),
        P("rep", None),
        P("rep", "fsdp", None),
        P("rep", "fsdp", None),
        P("rep", "fsdp", None),
        P(),
    )
    return jax.shard_map(
        local,
        mesh=mesh,
        in_specs=placed,
        out_specs=(P("rep", "fsdp", None), P("rep", "fsdp", None)),
        check_vma=False,
    )
```

time: 332 us -> 69.1 us (0.21)
  waiting for transfers between devices: 273 us -> 0 us
  Pallas kernels: 0 us -> 65.9 us
  starting transfers between devices: 22.7 us -> 0 us
  between operations: 14.8 us -> 1.3 us
  matrix products: 9.47 us -> 0 us
  local copies, waits for them, and re-layouts: 7.73 us -> 1.5 us
  other arithmetic: 3.94 us -> 0 us
    all_gather x2 -> x0, waiting for transfers between devices: 197 us -> none  [the longest x1 105 us: local(): lax.all_gather(weight, 'fsdp', axis=0, tiled=True)]
    all_to_all x1 -> x0, waiting for transfers between devices: 67.8 us -> none  [local(): lax.all_to_all(normed, 'fsdp', split_axis=1, concat_axis=0, tiled=True)]
    pallas_call x0 -> x1, Pallas kernels: none -> 65.9 us  [fused(): pl.pallas_call(partial(kernel, level), name=f'layer_level_{level}', out_s...]
    all_to_all x1 -> x0, starting transfers between devices: 19.4 us -> none  [local(): lax.all_to_all(normed, 'fsdp', split_axis=1, concat_axis=0, tiled=True)]
    dot_general x2 -> x0, matrix products: 9.47 us -> none  [the longest x1 5.39 us: local(): jnp.dot(normed, lax.all_gather(weight, 'fsdp', axis=0, tiled=True), prefe...]
    ppermute x1 -> x0, waiting for transfers between devices: 7.18 us -> none  [swapped(): return lax.ppermute(block, axis, route)]
    all_to_all x1 -> x0, local copies, waits for them, and re-layouts: 3.92 us -> none  [local(): lax.all_to_all(normed, 'fsdp', split_axis=1, concat_axis=0, tiled=True)]
  transfers between devices with their start and end apart: 4 -> 0, of which waited for: 4 -> 0; matrix products, arithmetic and copies ran while one was open for 5% -> 0% of each run, Pallas kernels for 0% -> 0%
where the time goes in v2:
time: 69.1 us; the launch traced here: 68.9 us
  Pallas kernels  65.9 us (95%)
  local copies, waits for them, and re-layouts  1.5 us (2%)
  between operations  1.3 us (2%)
    pallas_call x1, Pallas kernels, fused(): pl.pallas_call(partial(kernel, level), name=f'layer_level_{level}', out_s...  65.9 us
    unnamed x2, local copies, waits for them, and re-layouts  1.5 us

profile of v2, /device:TPU:1, one launch (start us, length us, event | category | flops | bytes accessed | tf_op | source)
XLA Modules:
  0.0 68.9 jit_solution(5298997781831828035)
XLA Ops:
  1.3 66.1 %conditional.1 = ((bf16[256,512]{1,0:T(8,128)(2,1)S(1)}, f32[256,512]{1,0:T(8,128)S(1)})) conditional(s32[]{:T(128)} %clamp.3, (bf16[256,4096]{1,0:T(8,128)(2,1)}, f32[1,4096]{1,0:T(1,128)}, bf16[256,512]{1,0:T(8,128)(2,1)}, bf16[256,512]{1,0:T(8,128)(2,1)}, f32[256,512]{1,0:T(8,128)}) %tuple.71, ...), branch_computations={%region_0.1_spmd, %region_1.2_spmd, %region_2.3_spmd, %region_3.4_... | conditional | bytes 8 | solution.py:371
  1.3 65.9 %layer_level_1.1 = (bf16[256,512]{1,0:T(8,128)(2,1)S(1)}, f32[256,512]{1,0:T(8,128)S(1)}) custom-call(bf16[256,4096]{1,0:T(8,128)(2,1)} %get-tuple-element.69.hid_ref, f32[1,4096]{1,0:T(1,128)} %get-tuple-element.70.gain_ref, bf16[256,512]{1,0:T(8,128)(2,1)} %get-tuple-element.71.w_ref, bf16[256,512]{1,0:T(8,128)(2,1)} %get-tuple-element.72.d_ref, ...), custom_call_target="tpu_custom_call" | custom-call | tf_op jit(solution)/shard_map/cond/branch_1_fun/layer_level_1/pallas_call | solution.py:328
  67.4 0.7 %copy.21 = bf16[1,256,512]{2,1,0:T(8,128)(2,1)} copy(bf16[1,256,512]{2,1,0:T(8,128)(2,1)S(1)} %bitcast.27) | data formatting | bytes 524288
  68.1 0.8 %copy.22 = f32[1,256,512]{2,1,0:T(8,128)} copy(f32[1,256,512]{2,1,0:T(8,128)S(1)} %bitcast.26) | data formatting | bytes 1048576

commit v3 on v2

--- a/solution.py
+++ b/solution.py
@@ -14,12 +14,10 @@
 N_Y = 4
 X_LEVELS = 2
 W_CHUNKS = 4
+STORE = True
 BACK = 2
-
-
-def copies_of(level):
-    common = W_CHUNKS + 4 + 6 + 3 * W_CHUNKS + BACK
-    return common + (22 + BACK if level < X_LEVELS else 12 + 3 * BACK)
+EARLY = 4
+N_SEND, N_RECV = 13, 32
 
 
 def kernel(
@@ -27,7 +25,7 @@
     hid, mom, normed, to_core, d, wts, part, vals_in,
     keep, keep_side, first_out, first_in, side_out, side_in, own_out, own_in,
     z_out, z_in, back_out, back_in,
-    local_sem, send_sem, recv_sem,
+    local_sem, send_sem, recv_sem, ready,
 ):
     along_x = level < X_LEVELS
     rows, feats = hid.shape
@@ -45,17 +43,28 @@
     across = at(rep, y, 1 - half, core)
     other = at(rep, y, half, 1 - core)
     pair = at(pair_rep, y, half, core)
-    friends = [up, down, across, other, pair]
+    friends, far_friends = [up, down, other, pair], [across]
     if along_x:
         pair_up, pair_down = at(pair_rep, y + 1, half, core), at(pair_rep, y - 1, half, core)
         friends = friends + [pair_up, pair_down]
     else:
         pair_across = at(pair_rep, y, 1 - half, core)
-        friends = friends + [pair_across]
+        far_friends = far_friends + [pair_across]
+
+    def signal(semaphore, devices):
+        for device in devices:
+            pl.semaphore_signal(semaphore, 1, device_id=device, device_id_type=MESH)
 
     barrier = pltpu.get_barrier_semaphore()
-    for device in friends:
-        pl.semaphore_signal(barrier, 1, device_id=device, device_id_type=MESH)
+    if along_x:
+        ahead = rep // N_X < EARLY
+        knows = jnp.logical_or(half == 1, jnp.logical_not(ahead))
+        pl.when(jnp.logical_or(half == 0, jnp.logical_not(ahead)))(
+            lambda: signal(barrier, far_friends)
+        )
+    else:
+        signal(barrier, far_friends)
+    signal(barrier, friends)
 
     def fetch(src, dst, i):
         copy = pltpu.make_async_copy(src, dst, local_sem.at[i])
@@ -65,28 +74,51 @@
     load_hid = fetch(hid_ref, hid, 0)
     load_d = fetch(d_ref, d.at[0], 1)
 
-    sent = []
-
-    def send(src, dst, device):
-        i = len(sent)
+    leaving, landing = {}, {}
+
+    def send(src, dst, device, leave, land, start=True):
         copy = pltpu.make_async_remote_copy(
-            src, dst, send_sem.at[i], recv_sem.at[i], device_id=device, device_id_type=MESH
+            src,
+            dst,
+            send_sem.at[leaving.setdefault(leave, len(leaving))],
+            recv_sem.at[landing.setdefault(land, len(landing))],
+            device_id=device,
+            device_id_type=MESH,
         )
-        copy.start()
-        sent.append(copy)
+        if start:
+            copy.start()
         return copy
 
-    pl.semaphore_wait(barrier, len(friends))
+    def landed(land, whole):
+        pltpu.make_async_copy(whole, whole, recv_sem.at[landing[land]]).wait()
+
+    if along_x:
+        pl.semaphore_wait(barrier, len(friends) + knows.astype(jnp.int32) * len(far_friends))
+        pl.when(jnp.logical_and(half == 1, ahead))(lambda: signal(ready, far_friends))
+    else:
+        pl.semaphore_wait(barrier, len(friends) + len(far_friends))
 
     def piece(q):
         n = blk // W_CHUNKS
         return pl.ds(q * n, n)
 
-    w_cross = [send(w_ref.at[piece(q)], wts.at[4, piece(q)], across) for q in range(W_CHUNKS)]
+    w_cross = [
+        send(w_ref.at[piece(q)], wts.at[4, piece(q)], across, "w", f"w{q}", start=False)
+        for q in range(W_CHUNKS)
+    ]
+
+    def start_w():
+        for copy in w_cross:
+            copy.start()
+
+    if along_x:
+        pl.when(knows)(start_w)
+    else:
+        start_w()
     load_w = fetch(w_ref, wts.at[0], 2)
     load_mom = fetch(mom_ref, mom, 3)
     load_d.wait()
-    core_d = send(d.at[0], d.at[1], other)
+    core_d = send(d.at[0], d.at[1], other, "d", "d")
 
     step = 32
 
@@ -111,8 +143,8 @@
     load_hid.wait()
     lax.fori_loop(0, rows // step, norm_rows, 0)
     core_n = {
-        1: send(to_core.at[1 - half], normed.at[1, 1 - half], other),
-        0: send(to_core.at[half], normed.at[1, half], other),
+        1: send(to_core.at[1 - half], normed.at[1, 1 - half], other, "n", "n1"),
+        0: send(to_core.at[half], normed.at[1, half], other, "n", "n0"),
     }
 
     def tokens_of(t, k, far):
@@ -128,26 +160,25 @@
 
     mine = pl.ds(pl.multiple_of(bit * mid, mid), mid)
     theirs = pl.ds(pl.multiple_of((1 - bit) * mid, mid), mid)
-    first, side, own = {}, {0: [], 1: []}, {}
+    first, own = {}, {}
 
     def send_side(far, way, part_of):
         src = side_out.at[far, way, part_of]
         if along_x:
             ends = ((up, down)[way], (pair_up, pair_down)[way])
             for i, span in enumerate((mine, theirs)):
-                side[far].append(
-                    send(src.at[span], side_in.at[far, way, part_of, pl.ds(i * mid, mid)], ends[i])
-                )
+                dst = side_in.at[far, way, part_of, pl.ds(i * mid, mid)]
+                send(src.at[span], dst, ends[i], "side", f"side{far}")
         else:
-            side[far].append(send(src, side_in.at[far, way, part_of], (up, down)[way]))
+            send(src, side_in.at[far, way, part_of], (up, down)[way], "side", f"side{far}")
 
     def reduce_first(far):
         block = grad_block(2, far).astype(BF16)
         first_out[far, 0] = block[:, :cols]
         first_out[far, 1] = block[:, cols:]
         first[far] = [
-            send(first_out.at[far, 0], first_in.at[far, 0], up),
-            send(first_out.at[far, 1], first_in.at[far, 1], down),
+            send(first_out.at[far, 0], first_in.at[far, 0], up, "first", f"first{far}0"),
+            send(first_out.at[far, 1], first_in.at[far, 1], down, "first", f"first{far}1"),
         ]
         for way, k in ((0, 1), (1, 3)):
             block = grad_block(k, far)
@@ -161,7 +192,7 @@
         keep[far] = block
         if along_x:
             own_out[far] = keep[far, theirs].astype(BF16)
-            own[far] = send(own_out.at[far], own_in.at[far], pair)
+            own[far] = send(own_out.at[far], own_in.at[far], pair, "own", f"own{far}")
 
     def reduce_second(far):
         for way in range(2):
@@ -181,8 +212,7 @@
         return total
 
     def wait_reduced(far):
-        for copy in side[far]:
-            copy.wait_recv()
+        landed(f"side{far}", side_in.at[far])
         if along_x:
             own[far].wait_recv()
 
@@ -205,118 +235,126 @@
     reduce_second(1)
     reduce_first(0)
 
+
+    def start_lower():
+        pl.semaphore_wait(ready, len(far_friends))
+        start_w()
+
+    if along_x:
+        pl.when(jnp.logical_not(knows))(start_lower)
     wait_reduced(1)
-    crossing = []
     if along_x:
         z_out[0] = (reduced(1, mine, (0, mid)) + own_in[1].astype(F32)).astype(BF16)
         for i in range(BACK):
-            crossing.append(send(z_out.at[0, back_rows(i)], z_in.at[0, back_rows(i)], across))
+            send(z_out.at[0, back_rows(i)], z_in.at[0, back_rows(i)], across, "z", f"z{i}")
     else:
         for i, span in enumerate((mine, theirs)):
             start = bit * mid if i == 0 else (1 - bit) * mid
             z_out[i] = reduced(1, span, (pl.multiple_of(start, mid),)).astype(BF16)
         for q in range(BACK):
             for i, device in enumerate((across, pair_across)):
-                crossing.append(send(z_out.at[i, back_rows(q)], z_in.at[i, back_rows(q)], device))
-
-    far_up, far_down, far_relay = {}, {}, []
+                send(z_out.at[i, back_rows(q)], z_in.at[i, back_rows(q)], device, "z", f"z{q}")
+
+    far_up, far_down = {}, {}
 
     def spread(q):
         w_cross[q].wait_recv()
         s = piece(q)
         for way in (q % 2, 1 - q % 2):
             if way == 0:
-                far_up[q] = send(wts.at[4, s], wts.at[7, s], up)
+                land = f"far{q}" if q % 2 == 0 else "far"
+                far_up[q] = send(wts.at[4, s], wts.at[7, s], up, "far", land)
             else:
-                far_down[q] = send(wts.at[4, s], wts.at[5, s], down)
+                land = f"far{q}" if q % 2 else "far"
+                far_down[q] = send(wts.at[4, s], wts.at[5, s], down, "far", land)
 
     def relay(q):
         s = piece(q)
         if q % 2 == 0:
             far_up[q].wait_recv()
-            far_relay.append(send(wts.at[7, s], wts.at[6, s], up))
+            send(wts.at[7, s], wts.at[6, s], up, "far_relay", "far_relay")
         else:
             far_down[q].wait_recv()
-            far_relay.append(send(wts.at[5, s], wts.at[6, s], down))
+            send(wts.at[5, s], wts.at[6, s], down, "far_relay", "far_relay")
 
     spread(0)
     reduce_second(0)
     lower, upper = pl.ds(0, mid), pl.ds(mid, mid)
-    near_up = [send(w_ref.at[s], wts.at[3, s], up) for s in (lower, upper)]
-    near_down = [send(w_ref.at[s], wts.at[1, s], down) for s in (upper, lower)]
+    for i, (s_up, s_down) in enumerate(((lower, upper), (upper, lower))):
+        send(w_ref.at[s_up], wts.at[3, s_up], up, "near", f"near{i}")
+        send(w_ref.at[s_down], wts.at[1, s_down], down, "near", f"near{i}")
     spread(1)
     relay(0)
     wait_reduced(0)
-    pair_near = []
     if along_x:
         keep[0, mine] = reduced(0, mine, (0, mid)) + own_in[0].astype(F32)
     else:
         z_out[2] = reduced(0, theirs, (pl.multiple_of((1 - bit) * mid, mid),)).astype(BF16)
         for q in range(BACK):
-            pair_near.append(send(z_out.at[2, back_rows(q)], z_in.at[2, back_rows(q)], pair))
+            send(z_out.at[2, back_rows(q)], z_in.at[2, back_rows(q)], pair, "z", f"z{q}")
         keep[0, mine] = reduced(0, mine, (pl.multiple_of(bit * mid, mid),))
-    near_up[0].wait_recv()
-    near_down[0].wait_recv()
-    near_relay = [
-        send(wts.at[3, lower], wts.at[2, lower], up),
-        send(wts.at[1, upper], wts.at[2, upper], down),
-    ]
+    landed("near0", wts.at[1])
+    send(wts.at[3, lower], wts.at[2, lower], up, "near_relay", "near_relay")
+    send(wts.at[1, upper], wts.at[2, upper], down, "near_relay", "near_relay")
     spread(2)
     relay(1)
-    near_up[1].wait_recv()
-    near_down[1].wait_recv()
+    landed("near1", wts.at[1])
     project(1, 0)
     project(3, 0)
     spread(3)
     relay(2)
     project(0, 1)
     relay(3)
-    for copy in near_relay:
-        copy.wait_recv()
+    landed("near_relay", wts.at[2])
     project(2, 0)
-    for q in range(W_CHUNKS):
-        if q % 2 == 0:
-            far_down[q].wait_recv()
-        else:
-            far_up[q].wait_recv()
+    landed("far", wts.at[5])
     project(1, 1)
     project(3, 1)
-
-    back = []
 
     def finish(q):
         s = back_rows(q)
         n = mid // BACK
         total = keep[0, pl.ds(pl.multiple_of(bit * mid + q * n, n), n)]
         if along_x:
-            crossing[q].wait_recv()
+            landed(f"z{q}", z_in.at[0, s])
             total = total + z_in[0, s].astype(F32)
         else:
-            crossing[2 * q].wait_recv()
-            crossing[2 * q + 1].wait_recv()
-            pair_near[q].wait_recv()
+            landed(f"z{q}", z_in.at[:, s])
             total = total + z_in[0, s].astype(F32) + z_in[1, s].astype(F32) + z_in[2, s].astype(F32)
         result = 0.5 * total
         back_out[s] = result.astype(BF16)
-        back.append(send(back_out.at[s], back_in.at[s], pair))
+        send(back_out.at[s], back_in.at[s], pair, "back", "back")
         averaged_ref[pl.ds(pl.multiple_of(bit * mid + q * n, n), n)] = result
 
-    for copy in far_relay:
-        copy.wait_recv()
+    landed("far_relay", wts.at[6])
     project(2, 1, tokens=(1,))
-    vals_send = send(part.at[1], vals_in, other)
+    vals_send = send(part.at[1], vals_in, other, "vals", "vals")
     project(2, 1, tokens=(0,))
     for q in range(BACK):
         finish(q)
     vals_send.wait_recv()
     values_ref[...] = (part[0] + vals_in[...]).astype(BF16)
-    for copy in back:
-        copy.wait_recv()
+    landed("back", back_in)
     averaged_ref[theirs] = back_in[...].astype(F32)
 
-    assert len(sent) == copies_of(level)
-    for copy in sent:
-        copy.wait_send()
+    total_of = {
+        "w": wts.at[4],
+        "d": d.at[0],
+        "n": to_core,
+        "first": first_out,
+        "side": side_out,
+        "own": own_out,
+        "z": z_out.at[0] if along_x else z_out,
+        "far": wts.at[pl.ds(4, 2)],
+        "far_relay": wts.at[6],
+        "near": wts.at[pl.ds(0, 2)],
+        "near_relay": wts.at[2],
+        "vals": vals_in,
+        "back": back_in,
+    }
+    assert len(leaving) <= N_SEND and len(landing) <= N_RECV
+    for leave, i in leaving.items():
+        pltpu.make_async_copy(total_of[leave], total_of[leave], send_sem.at[i]).wait()
 
 
 def fused(level, hidden, gain, weight, cotangent, momentum):
@@ -356,8 +394,9 @@
             pltpu.VMEM((mid, kv), BF16),
             pltpu.VMEM((mid, kv), BF16),
             pltpu.SemaphoreType.DMA((4,)),
-            pltpu.SemaphoreType.DMA((copies_of(level),)),
-            pltpu.SemaphoreType.DMA((copies_of(level),)),
+            pltpu.SemaphoreType.DMA((N_SEND,)),
+            pltpu.SemaphoreType.DMA((N_RECV,)),
+            pltpu.SemaphoreType.REGULAR,
         ],
         compiler_params=pltpu.CompilerParams(
             collective_id=level, has_side_effects=True, vmem_limit_bytes=40 << 20
@@ -365,12 +404,40 @@
     )(hidden, gain, weight, cotangent, momentum)
 
 
+def store_kernel(values_ref, averaged_ref, values_out, averaged_out, sems):
+    copies = [
+        pltpu.make_async_copy(values_ref, values_out, sems.at[0]),
+        pltpu.make_async_copy(averaged_ref, averaged_out, sems.at[1]),
+    ]
+    for copy in copies:
+        copy.start()
+    for copy in copies:
+        copy.wait()
+
+
+def store(values, averaged):
+    anywhere = pl.BlockSpec(memory_space=pl.ANY)
+    return pl.pallas_call(
+        store_kernel,
+        name="store",
+        out_shape=(
+            jax.ShapeDtypeStruct(values.shape, values.dtype),
+            jax.ShapeDtypeStruct(averaged.shape, averaged.dtype),
+        ),
+        in_specs=[anywhere, anywhere],
+        out_specs=(anywhere, anywhere),
+        scratch_shapes=[pltpu.SemaphoreType.DMA((2,))],
+    )(values, averaged)
+
+
 def local(hidden_in, norm_gain, w_value, d_values, momentum, step):
     levels = lax.axis_size("rep").bit_length() - 1
     branches = [partial(fused, level) for level in range(levels)]
     values, averaged = lax.switch(
-        step % levels, branches, hidden_in[0], norm_gain, w_value[0], d_values[0], momentum[0]
+        lax.rem(step, levels), branches, hidden_in[0], norm_gain, w_value[0], d_values[0], momentum[0]
     )
+    if STORE:
+        values, averaged = store(values, averaged)
     return (values[None], averaged[None])
 
 

time: 69.1 us -> 68.6 us (level)
  the two profiles are of different devices: /device:TPU:1 before, /device:TPU:332 now
where the time goes in v3:
time: 68.6 us; the launch traced here: 68.4 us
  Pallas kernels  66.6 us (97%)
  between operations  1.47 us (2%)
    pallas_call x1, Pallas kernels, fused(): pl.pallas_call(partial(kernel, level), name=f'layer_level_{level}', out_s...  65.7 us

profile of v3, /device:TPU:332, one launch (start us, length us, event | category | flops | bytes accessed | tf_op | source)
XLA Modules:
  0.0 68.4 jit_solution(15346752193869271252)
XLA Ops:
  1.3 66.0 %conditional.1 = ((bf16[256,512]{1,0:T(8,128)(2,1)S(1)}, f32[256,512]{1,0:T(8,128)S(1)})) conditional(s32[]{:T(128)} %clamp.3, (bf16[256,4096]{1,0:T(8,128)(2,1)}, f32[1,4096]{1,0:T(1,128)}, bf16[256,512]{1,0:T(8,128)(2,1)}, bf16[256,512]{1,0:T(8,128)(2,1)}, f32[256,512]{1,0:T(8,128)}) %tuple.50, ...), branch_computations={%region_0.0_spmd, %region_1.0_spmd, %region_2.0_spmd, %region_3.0_... | conditional | bytes 8 | solution.py:436
  1.3 65.7 %layer_level_1.1 = (bf16[256,512]{1,0:T(8,128)(2,1)S(1)}, f32[256,512]{1,0:T(8,128)S(1)}) custom-call(bf16[256,4096]{1,0:T(8,128)(2,1)} %get-tuple-element.55.hid_ref, f32[1,4096]{1,0:T(1,128)} %get-tuple-element.56.gain_ref, bf16[256,512]{1,0:T(8,128)(2,1)} %get-tuple-element.57.w_ref, bf16[256,512]{1,0:T(8,128)(2,1)} %get-tuple-element.58.d_ref, ...), custom_call_target="tpu_custom_call" | custom-call | tf_op jit(solution)/shard_map/cond/branch_1_fun/layer_level_1/pallas_call | solution.py:366
  67.3 0.9 %store.1 = (bf16[256,512]{1,0:T(8,128)(2,1)}, f32[256,512]{1,0:T(8,128)}) custom-call(bf16[256,512]{1,0:T(8,128)(2,1)S(1)} %get-tuple-element.81.values_ref, f32[256,512]{1,0:T(8,128)S(1)} %get-tuple-element.82.averaged_ref), custom_call_target="tpu_custom_call" | custom-call | tf_op jit(solution)/shard_map/store/pallas_call | solution.py:420
